TPU v7x, 32 devices: a whole 2x2x4 slice. The times are simulated.
32 devices in a mesh: group: 2 (over y), outer: 4 (over z), blk: 2 (over x), hid: 2 (over core).
Axes of the slice: x: 2, y: 2, z: 4, core: 2. Of those that a mesh axis runs over, the one named last changes fastest.
Arguments:
- tokens: bfloat16 [2048, 3584], P(('group', 'outer', 'blk')), parts along dimension 0, may hold values from -6 to 6
- routes: int32 [2048, 2], P(('group', 'outer', 'blk')), parts along dimension 0, may hold values from 0 to 3, all different within a row; in each aligned block of 128 rows (0 to 127, 128 to 255, ...) at most 80 rows name the same one
- scores: float32 [2048, 2], P(('group', 'outer', 'blk')), parts along dimension 0, may hold values from 0.1 to 1
- gate_weight: bfloat16 [4, 2048, 3584], P('outer', ('blk', 'hid')), may hold values from -0.09375 to 0.09375
- up_weight: bfloat16 [4, 2048, 3584], P('outer', ('blk', 'hid')), may hold values from -0.09375 to 0.09375
- down_weight: bfloat16 [4, 2048, 3584], P('outer', ('blk', 'hid')), may hold values from -0.125 to 0.125
Outputs:
- mixed: bfloat16 [2048, 3584], P(('group', 'outer', 'blk'), 'hid'), parts along dimension 0
There are 2 independent parts, one for each index of `group`. A program takes and returns all parts, laid end to end along the dimension named above; an argument that names none is the same for every part. Nothing has to cross between parts.
Inputs may be any that keep to these rules, and one draw needn't show every extreme that they name: `routes`: each token names 2 different experts. In the rows of one device (aligned blocks of 128 tokens) no expert is named more than 80 times, and in some blocks of every draw some expert is named exactly 80 times.
All inputs are finite; a program needn't handle non-finite values.
Results may differ from a plain program's by a relative error of at most 0.0067.
Values may be sent and summed in bfloat16 or wider, within the bound.
A program may use at most 128 MiB of HBM per device.

v0:
```python
import jax
import jax.numpy as jnp
from jax import lax
from jax.sharding import PartitionSpec as P

route_scale = 2.5


def slice_terms(rows, gate_piece, up_piece, down_piece):
    dims = (((1,), (1,)), ((), ()))
    gate_part = lax.dot_general(rows, gate_piece, dims, preferred_element_type=jnp.float32)
    up_part = lax.dot_general(rows, up_piece, dims, preferred_element_type=jnp.float32)
    hidden = (jax.nn.silu(gate_part) * up_part).astype(jnp.bfloat16)
    return jnp.dot(hidden, down_piece, preferred_element_type=jnp.float32)


def local(tokens, routes, scores, gate_weight, up_weight, down_weight):
    tok_dev, width = tokens.shape
    topk = routes.shape[1]
    experts = lax.axis_size("outer")
    shares = lax.axis_size("hid")
    half = width // shares
    capacity = (tok_dev * topk * 5 // experts + 3) // 4
    flat = routes.reshape(-1)
    onehot = (flat[:, None] == jnp.arange(experts, dtype=jnp.int32)[None, :]).astype(jnp.int32)
    before = jnp.cumsum(onehot, axis=0) - onehot
    rank = jnp.sum(before * onehot, axis=1)
    slots = flat * capacity + rank
    owner = jnp.arange(tok_dev * topk, dtype=jnp.int32) // topk
    columns = tokens.shape[1]
    send = jnp.zeros((experts * capacity, columns), jnp.bfloat16).at[slots].set(tokens[owner])
    send = send.reshape(experts, capacity, columns)
    gate_local = gate_weight[0]
    up_local = up_weight[0]
    down_local = down_weight[0]
    arrived = lax.all_to_all(send, "outer", split_axis=0, concat_axis=0, tiled=True)
    senders, count, unused = arrived.shape
    rows = arrived.reshape(senders * count, width)
    total = slice_terms(
        rows,
        lax.all_gather(gate_local, "blk", axis=0, tiled=True),
        lax.all_gather(up_local, "blk", axis=0, tiled=True),
        lax.all_gather(down_local, "blk", axis=0, tiled=True),
    )
    summed = lax.psum(total.astype(jnp.bfloat16), "hid").astype(jnp.float32)
    share = lax.dynamic_slice_in_dim(summed, lax.axis_index("hid") * half, half, 1)
    answered = share.astype(jnp.bfloat16).reshape(senders, count, half)
    returned = lax.all_to_all(answered, "outer", split_axis=0, concat_axis=0, tiled=True)
    picked = (
        returned.reshape(experts * capacity, half)[slots]
        .astype(jnp.float32)
        .reshape(tok_dev, topk, half)
    )
    weights = route_scale * scores / jnp.sum(scores, axis=1, keepdims=True)
    mixed = jnp.sum(weights[:, :, None] * picked, axis=1)
    return mixed.astype(jnp.bfloat16)


def solution(mesh):
    in_specs = (
        P(("group", "outer", "blk"), None),
        P(("group", "outer", "blk"), None),
        P(("group", "outer", "blk"), None),
        P("outer", ("blk", "hid"), None),
        P("outer", ("blk", "hid"), None),
        P("outer", ("blk", "hid"), None),
    )
    out_specs = P(("group", "outer", "blk"), "hid")
    return jax.shard_map(local, mesh=mesh, in_specs=in_specs, out_specs=out_specs, check_vma=False)
```

profile of v0, /device:TPU:0, one launch (start us, length us, event | category | flops | bytes accessed | tf_op | source)
XLA Modules:
  0.0 375.0 jit_solution(7027651566630963961)
XLA Ops:
  6.5 0.7 all-gather.7.cloned.1.call-update
  7.3 0.7 all-gather.11.cloned.1.call-update
  8.1 0.7 all-gather.9.cloned.1.call-update
  8.8 0.1 copy.12
  8.9 0.1 eq.29
  9.1 0.1 eq.25
  9.2 1.2 reduce-window.6
  10.8 0.1 copy.11
  10.9 0.1 mul.48
  11.2 9.2 %scatter_custom_fusion = bf16[320,3584]{1,0:T(8,128)(2,1)S(1)} fusion(s32[256]{0:T(256)S(1)} %bitcast.49, bf16[128,3584]{1,0:T(8,128)(2,1)S(1)} %copy-done, s32[1024]{0:T(1024)S(1)} %pad_clamp_fusion.1, bf16[]{:T(256)} %constant.34.clone.1), kind=kCustom, calls=%fused_computation.11 | custom fusion | bytes 2293762 | tf_op jit(solution)/shard_map/scatter | solution.py:31
  20.4 58.6 %all_to_all.10 = bf16[4,80,3584]{2,1,0:T(8,128)(2,1)} all-to-all(bf16[4,80,3584]{2,1,0:T(8,128)(2,1)S(1)} %bitcast.46), channel_id=1, replica_groups=mesh['group'=2,'outer'=4,'blk'=2,'hid'=2] {'outer'}, dimensions={0} | all-to-all | bytes 4587520 | tf_op jit(solution)/shard_map/all_to_all | solution.py:36
  79.0 24.8 %all-gather.7.cloned.1.call-done = bf16[1,1024,3584]{2,1,0:T(8,128)(2,1)} async-done(((bf16[1,512,3584]{2,1,0:T(8,128)(2,1)}), bf16[1,1024,3584]{2,1,0:T(8,128)(2,1)}) %all-gather.7.cloned.1.call-update) | async-done | bytes 7340048 | tf_op jit(solution)/shard_map/all_gather | solution.py:41
  103.8 7.6 %fusion.4 = f32[320,1024]{1,0:T(8,128)} fusion(bf16[320,3584]{1,0:T(8,128)(2,1)} %bitcast.47, bf16[1,1024,3584]{2,1,0:T(8,128)(2,1)} %all-gather.7.cloned.1.call-done), kind=kOutput, calls=%fused_computation.7 | convolution fusion | flops 2348810240 | bytes 10944512 | tf_op jit(solution)/shard_map/dot_general | solution.py:11
  111.5 86.1 %all-gather.11.cloned.1.call-done = bf16[1,1024,3584]{2,1,0:T(8,128)(2,1)} async-done(((bf16[1,512,3584]{2,1,0:T(8,128)(2,1)}), bf16[1,1024,3584]{2,1,0:T(8,128)(2,1)}) %all-gather.11.cloned.1.call-update) | async-done | bytes 7340048 | tf_op jit(solution)/shard_map/all_gather | solution.py:43
  197.6 93.8 %all-gather.9.cloned.1.call-done = bf16[1,1024,3584]{2,1,0:T(8,128)(2,1)} async-done(((bf16[1,512,3584]{2,1,0:T(8,128)(2,1)}), bf16[1,1024,3584]{2,1,0:T(8,128)(2,1)}) %all-gather.9.cloned.1.call-update) | async-done | bytes 7340048 | tf_op jit(solution)/shard_map/all_gather | solution.py:42
  291.4 11.9 %fusion.6 = bf16[320,3584]{1,0:T(8,128)(2,1)} fusion(bf16[1,1024,3584]{2,1,0:T(8,128)(2,1)} %all-gather.11.cloned.1.call-done, bf16[320,3584]{1,0:T(8,128)(2,1)S(1)} %bitcast.48, bf16[1,1024,3584]{2,1,0:T(8,128)(2,1)} %all-gather.9.cloned.1.call-done, f32[320,1024]{1,0:T(8,128)} %fusion.4), kind=kOutput, calls=%fused_computation.9 | convolution fusion | flops 4700733440 | bytes 20578304 | tf_op jit(solution)/shard_map/dot_general | solution.py:14
  303.3 21.7 %all-reduce.2.cloned.1.call-done = bf16[320,3584]{1,0:T(8,128)(2,1)} async-done(((bf16[320,3584]{1,0:T(8,128)(2,1)}), bf16[320,3584]{1,0:T(8,128)(2,1)}) %all-reduce.2.cloned.1.call-update) | async-done | bytes 2293776 | tf_op jit(solution)/shard_map/psum | solution.py:45
  325.0 2.3 convert_convert_fusion
  327.3 4.9 %all-to-all-start.1 = ((bf16[4,80,1792]{2,1,0:T(8,128)(2,1)}), bf16[4,80,1792]{2,1,0:T(8,128)(2,1)S(1)}, u32[]{:S(2)}, u32[]{:S(2)}) async-start(bf16[4,80,1792]{2,1,0:T(8,128)(2,1)} %bitcast.10), calls=%async_computation.1 | async-start | bytes 2293760 | tf_op jit(solution)/shard_map/all_to_all | solution.py:48
  332.2 0.1 copy.10
  332.3 28.1 %all-to-all-done.1 = bf16[4,80,1792]{2,1,0:T(8,128)(2,1)S(1)} async-done(((bf16[4,80,1792]{2,1,0:T(8,128)(2,1)}), bf16[4,80,1792]{2,1,0:T(8,128)(2,1)S(1)}, u32[]{:S(2)}, u32[]{:S(2)}) %all-to-all-start.1) | async-done | bytes 1146912 | tf_op jit(solution)/shard_map/all_to_all | solution.py:48
  360.5 2.3 gather_fusion
  362.7 2.3 reshape.112
  365.1 3.3 multiply_reduce_fusion
  (28 shorter events, 0.6 us)
Async XLA Ops:
  6.5 4.6 %copy-start = (bf16[128,3584]{1,0:T(8,128)(2,1)S(1)}, bf16[128,3584]{1,0:T(8,128)(2,1)}, u32[]{:S(2)}) copy-start(bf16[128,3584]{1,0:T(8,128)(2,1)} %param.6) | copy-start | bytes 2752516
  6.5 97.3 %all-gather.7.cloned.1.call-start = ((), (), s32[]{:S(2)}) async-start(), calls=%async_computation.3 | async-start | bytes 11010048 | tf_op jit(solution)/shard_map/all_gather | solution.py:41
  7.3 190.3 %all-gather.11.cloned.1.call-start = ((), (), s32[]{:S(2)}) async-start(), calls=%async_computation.5 | async-start | bytes 11010048 | tf_op jit(solution)/shard_map/all_gather | solution.py:43
  8.0 0.8 copy-start.2
  8.0 283.4 %all-gather.9.cloned.1.call-start = ((), (), s32[]{:S(2)}) async-start(), calls=%async_computation.4 | async-start | bytes 11010048 | tf_op jit(solution)/shard_map/all_gather | solution.py:42
  8.8 316.2 %all-reduce.2.cloned.1.call-start = ((), (), s32[]{:S(2)}) async-start(), calls=%async_computation.2 | async-start | bytes 4587520 | tf_op jit(solution)/shard_map/psum | solution.py:45
  103.8 187.5 %copy-start.1 = (bf16[4,80,3584]{2,1,0:T(8,128)(2,1)S(1)}, bf16[4,80,3584]{2,1,0:T(8,128)(2,1)}, u32[]{:S(2)}) copy-start(bf16[4,80,3584]{2,1,0:T(8,128)(2,1)} %all_to_all.10) | copy-start | bytes 6881284
  303.3 28.9 %copy-start.3 = (f32[128,2]{0,1:T(2,128)S(1)}, f32[128,2]{0,1:T(2,128)}, u32[]{:S(2)}) copy-start(f32[128,2]{0,1:T(2,128)} %param.8) | copy-start | bytes 3076
  327.3 33.2 %all-to-all-start.1 = ((bf16[4,80,1792]{2,1,0:T(8,128)(2,1)}), bf16[4,80,1792]{2,1,0:T(8,128)(2,1)S(1)}, u32[]{:S(2)}, u32[]{:S(2)}) async-start(bf16[4,80,1792]{2,1,0:T(8,128)(2,1)} %bitcast.10), calls=%async_computation.1 | async-start | bytes 2293760 | tf_op jit(solution)/shard_map/all_to_all | solution.py:48
Sparse Core Ops, SparseCore 0:
  8.9 94.8 all-gather.6
  105.4 92.1 all-gather.10
  199.1 92.1 all-gather.8
  303.4 21.5 all-reduce.1
where the time goes:
time: 375 us
  waiting for transfers between devices  257 us (69%)
  blocking collectives  58.6 us (16%)
  matrix products  19.5 us (5%)
  local copies, waits for them, and re-layouts  14.9 us (4%)
  between operations  13.2 us (4%)
  other arithmetic  7.1 us (2%)
  starting transfers between devices  4.98 us (1%)
    all_gather x1, waiting for transfers between devices, local(): lax.all_gather(up_local, 'blk', axis=0, tiled=True)  93.8 us
    all_gather x1, waiting for transfers between devices, local(): lax.all_gather(down_local, 'blk', axis=0, tiled=True)  86.1 us
    all_to_all x1, blocking collectives, local(): lax.all_to_all(send, 'outer', split_axis=0, concat_axis=0, tiled=True)  58.6 us
    all_to_all x1, waiting for transfers between devices, local(): lax.all_to_all(answered, 'outer', split_axis=0, concat_axis=0, tiled=True)  28.1 us
    all_gather x1, waiting for transfers between devices, local(): lax.all_gather(gate_local, 'blk', axis=0, tiled=True)  24.8 us
    psum x1, waiting for transfers between devices, local(): summed = lax.psum(total.astype(jnp.bfloat16), 'hid').astype(jnp.float32)  21.7 us
    dot_general x1, matrix products, slice_terms(): return jnp.dot(hidden, down_piece, preferred_element_type=jnp.float32)  11.9 us
    scatter x1, local copies, waits for them, and re-layouts, local(): jnp.zeros((experts * capacity, columns), jnp.bfloat16).at[slots]  9.2 us
  transfers between devices with their start and end apart: 5, of which 5 were waited for; matrix products, arithmetic and copies ran while one was open for 5% of the time, Pallas kernels for 0%

commit v1 on v0

--- a/solution.py
+++ b/solution.py
@@ -1,9 +1,16 @@
+import functools
 import jax
 import jax.numpy as jnp
 from jax import lax
+from jax.experimental import pallas as pl
+from jax.experimental.pallas import tpu as pltpu
 from jax.sharding import PartitionSpec as P
 
 route_scale = 2.5
+PIECES = 7
+WINDOW = 2
+ROUND_PARTS = (1,)
+SEND_ORDER = (2, 3, 1)
 
 
 def slice_terms(rows, gate_piece, up_piece, down_piece):
@@ -56,6 +63,279 @@
     return mixed.astype(jnp.bfloat16)
 
 
+MESH = pl.DeviceIdType.MESH
+bf16, f32 = jnp.bfloat16, jnp.float32
+
+
+def partner(z, d):
+    if d == 1:
+        return z + 1 - 2 * lax.rem(z, 2)
+    if d == 2:
+        return lax.rem(z + 2, 4)
+    if d == 3:
+        return 3 - z
+    return z
+
+
+def layer_kernel(rounds, pieces, tok, routes, scores, gate_hbm, up_hbm, down_hbm, out,
+                 tokv, gw, uw, dw, buffers, local_sem, z_s, z_r, sem_s, sem_r, back_s, back_r):
+    z, x, h = lax.axis_index("outer"), lax.axis_index("blk"), lax.axis_index("hid")
+    steps = buffers[0]["send"].shape[1]
+    half, units = tokv.shape[1], gw.shape[0]
+    piece = half // pieces
+    ox, oh = 1 - x, 1 - h
+    col0 = pl.multiple_of(h * half, 128)
+
+    load_tok = pltpu.make_async_copy(tok.at[:, pl.ds(col0, half)], tokv, local_sem.at[0])
+    load_tok.start()
+    loads = [
+        pltpu.make_async_copy(src.at[0], dst, local_sem.at[1 + i])
+        for i, (src, dst) in enumerate(((gate_hbm, gw), (up_hbm, uw), (down_hbm, dw)))
+    ]
+
+    barrier = pltpu.get_barrier_semaphore()
+    peers = [{"outer": partner(z, d)} for d in range(1, steps)] + [{"blk": ox}, {"hid": oh}]
+    for peer in peers:
+        pl.semaphore_signal(barrier, inc=1, device_id=peer, device_id_type=MESH)
+
+    tokens = routes.shape[0]
+    below = lax.broadcasted_iota(jnp.int32, (tokens, tokens), 1) < lax.broadcasted_iota(
+        jnp.int32, (tokens, tokens), 0)
+    below = jnp.where(below, 1.0, 0.0).astype(bf16)
+    weight = route_scale * scores[...] / (scores[:, 0:1] + scores[:, 1:2])
+    places, mixes = [], []
+    start = 0
+    for c in rounds:
+        wide = (tokens, steps * c)
+        lane = lax.broadcasted_iota(jnp.int32, wide, 1)
+        expert = lane // c
+        first = routes[:, 0:1] == expert
+        second = routes[:, 1:2] == expert
+        named = jnp.where(first | second, 1.0, 0.0)
+        rank = jnp.dot(below, named.astype(bf16), preferred_element_type=f32)
+        slot = (lane - expert * c + start).astype(f32)
+        place = jnp.where(rank == slot, named, 0.0)
+        mix = place * (jnp.where(first, weight[:, 0:1], 0.0) + jnp.where(second, weight[:, 1:2], 0.0))
+        mix_high = mix.astype(bf16)
+        places.append(place.astype(bf16))
+        mixes.append((mix_high, (mix - mix_high.astype(f32)).astype(bf16)))
+        start += c
+
+    where = [partner(z, d) for d in range(steps)]
+
+    def remote(src, dst, send_sem, recv_sem, peer):
+        return pltpu.make_async_remote_copy(
+            src_ref=src, dst_ref=dst, send_sem=send_sem, recv_sem=recv_sem,
+            device_id=peer, device_id_type=MESH)
+
+    work = [(r, p) for r in range(len(rounds)) for p in range(pieces)]
+    to_expert, across, beside, beside2, sum_hid, sum_blk, back = {}, {}, {}, {}, {}, {}, {}
+    for n, (r, p) in enumerate(work):
+        bufs, key = buffers[r], (r, p)
+        rows = bufs["rows"]
+        to_expert[key] = [
+            remote(bufs["send"].at[p, where[d]], rows.at[p, h, x, z], z_s.at[n, d], z_r.at[n, d], {"outer": where[d]})
+            for d in SEND_ORDER]
+        across[key] = remote(rows.at[p, h, x], rows.at[p, h, x], sem_s.at[0, n], sem_r.at[0, n], {"blk": ox})
+        beside[key] = remote(rows.at[p, h, x], rows.at[p, h, x], sem_s.at[1, n], sem_r.at[1, n], {"hid": oh})
+        beside2[key] = remote(rows.at[p, h, ox], rows.at[p, h, ox], sem_s.at[2, n], sem_r.at[2, n], {"hid": oh})
+        sum_hid[key] = remote(bufs["a_send"].at[p], bufs["a_recv"].at[p], sem_s.at[3, n], sem_r.at[3, n], {"hid": oh})
+        sum_blk[key] = remote(bufs["b_send"].at[p], bufs["b_recv"].at[p], sem_s.at[4, n], sem_r.at[4, n], {"blk": ox})
+        back[key] = [
+            remote(bufs["c_send"].at[p, where[d]], bufs["ret"].at[p, z], back_s.at[n, d], back_r.at[n, d], {"outer": where[d]})
+            for d in SEND_ORDER]
+
+    load_tok.wait()
+
+    def build(r, p):
+        sent = lax.dot_general(
+            places[r], tokv[:, p * piece:(p + 1) * piece], (((0,), (0,)), ((), ())), preferred_element_type=f32)
+        buffers[r]["send"][p] = sent.astype(bf16).reshape(steps, rounds[r], piece)
+        if (r, p) == work[0]:
+            pl.semaphore_wait(barrier, len(peers))
+        if work.index((r, p)) < WINDOW:
+            for copy in to_expert[r, p]:
+                copy.start()
+        buffers[r]["rows"][p, h, x, z] = buffers[r]["send"][p, z]
+
+    def forward(r, p):
+        n = work.index((r, p)) + WINDOW
+        if n < len(work):
+            for copy in to_expert[work[n]]:
+                copy.start()
+        for copy in to_expert[r, p]:
+            copy.wait_recv()
+        across[r, p].start()
+        beside[r, p].start()
+
+    def forward2(r, p):
+        across[r, p].wait_recv()
+        beside2[r, p].start()
+
+    nt = (((1,), (1,)), ((), ()))
+
+    def compute(r, p):
+        bufs = buffers[r]
+        rows, gate, up = bufs["rows"], bufs["gate"], bufs["up"]
+        beside[r, p].wait_recv()
+        beside2[r, p].wait_recv()
+        if (r, p) == work[0]:
+            loads[0].wait()
+            loads[1].wait()
+        parts = [rows[p, k].reshape(gate.shape[0], piece) for k in range(2)]
+
+        @pl.loop(0, units // 256)
+        def _(j):
+            take = pl.ds(pl.multiple_of(j * 256, 256), 256)
+            for total, weights in ((gate, gw), (up, uw)):
+                value = sum(
+                    lax.dot_general(
+                        parts[k], weights[take, k * half + p * piece:k * half + (p + 1) * piece], nt,
+                        preferred_element_type=f32)
+                    for k in range(2))
+                total[:, take] = value if p == 0 else total[:, take] + value
+
+    def activate(r, p):
+        bufs = buffers[r]
+        gate, up, hidden = bufs["gate"], bufs["up"], bufs["hidden"]
+
+        @pl.loop(0, gate.shape[0] // 32)
+        def _(j):
+            take = pl.ds(pl.multiple_of(j * 32, 32), 32)
+            value = gate[take, :]
+            hidden[take, :] = (value / (1.0 + jnp.exp(-value)) * up[take, :]).astype(bf16)
+
+        if r == 0:
+            loads[2].wait()
+
+    def down(r, p):
+        bufs = buffers[r]
+        shape = bufs["own"].shape[1:]
+        other = pl.ds(pl.multiple_of(oh * half + p * piece, 128), piece)
+        mine = pl.ds(pl.multiple_of(h * half + p * piece, 128), piece)
+        bufs["a_send"][p] = jnp.dot(
+            bufs["hidden"][...], dw[:, other], preferred_element_type=f32).astype(bf16).reshape(shape)
+        sum_hid[r, p].start()
+        bufs["own"][p] = jnp.dot(bufs["hidden"][...], dw[:, mine], preferred_element_type=f32).reshape(shape)
+
+    def reduce_hid(r, p):
+        bufs = buffers[r]
+        sum_hid[r, p].wait_recv()
+        bufs["b_send"][p] = (bufs["own"][p, ox] + bufs["a_recv"][p, ox].astype(f32)).astype(bf16)
+        sum_blk[r, p].start()
+        bufs["own"][p, x] = bufs["own"][p, x] + bufs["a_recv"][p, x].astype(f32)
+
+    def reduce_blk(r, p):
+        bufs = buffers[r]
+        sum_blk[r, p].wait_recv()
+        total = (bufs["own"][p, x] + bufs["b_recv"][p].astype(f32)).astype(bf16)
+        bufs["c_send"][p] = total.reshape(bufs["c_send"].shape[1:])
+        for copy in back[r, p]:
+            copy.start()
+        bufs["ret"][p, z] = bufs["c_send"][p, z]
+
+    def combine(r, p):
+        if r < len(rounds) - 1:
+            return
+        value = None
+        for q in range(len(rounds)):
+            for copy in back[q, p]:
+                copy.wait_recv()
+            result = buffers[q]["ret"][p].reshape(steps * rounds[q], piece)
+            for mix in mixes[q]:
+                term = jnp.dot(mix, result, preferred_element_type=f32)
+                value = term if value is None else value + term
+        out[:, p * piece:(p + 1) * piece] = value.astype(bf16)
+
+    def staggered(r, stages):
+        lines = []
+        for i in range(pieces + len(stages) - 1):
+            lines.append([(f, r, i - k) for k, f in enumerate(stages) if 0 <= i - k < pieces])
+        return lines
+
+    going = [staggered(r, (forward, forward2, compute)) for r in range(len(rounds))]
+    coming = [staggered(r, (down, reduce_hid, reduce_blk, combine)) for r in range(len(rounds))]
+    plan = [(build, 0, p) for p in range(pieces)]
+    for load in loads:
+        plan.append((lambda r, p, load=load: load.start(), 0, 0))
+    plan += [(build, r, p) for r in range(1, len(rounds)) for p in range(pieces)]
+    for r in range(len(rounds) + 1):
+        go = going[r] if r < len(rounds) else []
+        come = coming[r - 1] if r else []
+        for i in range(max(len(go), len(come))):
+            plan += (go[i] if i < len(go) else []) + (come[i] if i < len(come) else [])
+        if r < len(rounds):
+            plan.append((activate, r, 0))
+    for function, r, p in plan:
+        function(r, p)
+
+    for key in work:
+        for copy in to_expert[key] + back[key]:
+            copy.wait_send()
+        for group in (across, beside, beside2, sum_hid, sum_blk):
+            group[key].wait_send()
+
+
+def local_kernel(tokens, routes, scores, gate_weight, up_weight, down_weight):
+    tok_dev, width = tokens.shape
+    steps = lax.axis_size("outer")
+    half = width // 2
+    units = gate_weight.shape[1]
+    capacity = (tok_dev * routes.shape[1] * 5 // steps + 3) // 4
+    blocks = (capacity + 15) // 16
+    rounds, left = [], blocks
+    for part in range(len(ROUND_PARTS)):
+        take = left if part == len(ROUND_PARTS) - 1 else blocks * ROUND_PARTS[part] // sum(ROUND_PARTS)
+        rounds.append(16 * take)
+        left -= take
+    pieces = PIECES
+    piece = half // pieces
+    vmem, hbm = pl.BlockSpec(memory_space=pltpu.VMEM), pl.BlockSpec(memory_space=pl.ANY)
+    buffers = []
+    for c in rounds:
+        buffers.append({
+            "send": pltpu.VMEM((pieces, steps, c, piece), bf16),
+            "rows": pltpu.VMEM((pieces, 2, 2, steps, c, piece), bf16),
+            "gate": pltpu.VMEM((2 * steps * c, units), f32),
+            "up": pltpu.VMEM((2 * steps * c, units), f32),
+            "hidden": pltpu.VMEM((2 * steps * c, units), bf16),
+            "own": pltpu.VMEM((pieces, 2, steps * c, piece), f32),
+            "a_send": pltpu.VMEM((pieces, 2, steps * c, piece), bf16),
+            "a_recv": pltpu.VMEM((pieces, 2, steps * c, piece), bf16),
+            "b_send": pltpu.VMEM((pieces, steps * c, piece), bf16),
+            "b_recv": pltpu.VMEM((pieces, steps * c, piece), bf16),
+            "c_send": pltpu.VMEM((pieces, steps, c, piece), bf16),
+            "ret": pltpu.VMEM((pieces, steps, c, piece), bf16),
+        })
+    number = len(rounds) * pieces
+    dma = pltpu.SemaphoreType.DMA
+    scratch = [
+        pltpu.VMEM((tok_dev, half), bf16),
+        pltpu.VMEM((units, width), bf16),
+        pltpu.VMEM((units, width), bf16),
+        pltpu.VMEM((units, width), bf16),
+        buffers,
+        dma((4,)),
+        dma((number, steps)),
+        dma((number, steps)),
+        dma((5, number)),
+        dma((5, number)),
+        dma((number, steps)),
+        dma((number, steps)),
+    ]
+    macs = 6 * steps * sum(rounds) * units * width
+    return pl.pallas_call(
+        functools.partial(layer_kernel, tuple(rounds), pieces),
+        out_shape=jax.ShapeDtypeStruct((tok_dev, half), bf16),
+        in_specs=[hbm, vmem, vmem, hbm, hbm, hbm],
+        out_specs=vmem,
+        scratch_shapes=scratch,
+        compiler_params=pltpu.CompilerParams(
+            collective_id=0, has_side_effects=True, vmem_limit_bytes=56 * 1024 * 1024),
+        cost_estimate=pl.CostEstimate(flops=2 * macs, bytes_accessed=6 * units * width, transcendentals=0),
+    )(tokens, routes, scores, gate_weight, up_weight, down_weight)
+
+
 def solution(mesh):
     in_specs = (
         P(("group", "outer", "blk"), None),
@@ -66,4 +346,6 @@
         P("outer", ("blk", "hid"), None),
     )
     out_specs = P(("group", "outer", "blk"), "hid")
-    return jax.shard_map(local, mesh=mesh, in_specs=in_specs, out_specs=out_specs, check_vma=False)
+    fits = mesh.shape["outer"] == 4 and mesh.shape["blk"] == 2 and mesh.shape["hid"] == 2
+    body = local_kernel if fits else local
+    return jax.shard_map(body, mesh=mesh, in_specs=in_specs, out_specs=out_specs, check_vma=False)

time: 375 us -> 86.1 us (0.23)
  waiting for transfers between devices: 257 us -> 0 us
  Pallas kernels: 0 us -> 81.2 us
  blocking collectives: 58.6 us -> 0 us
  matrix products: 19.5 us -> 0 us
  between operations: 13.2 us -> 0.01 us
  local copies, waits for them, and re-layouts: 14.9 us -> 4.63 us
  other arithmetic: 7.1 us -> 0 us
  starting transfers between devices: 4.98 us -> 0 us
    all_gather x3 -> x0, waiting for transfers between devices: 205 us -> none  [the longest x1 93.8 us: local(): lax.all_gather(up_local, 'blk', axis=0, tiled=True)]
    pallas_call x0 -> x1, Pallas kernels: none -> 81.2 us  [local_kernel(): pl.pallas_call(functools.partial(layer_kernel, tuple(rounds), pieces), ou...]
    all_to_all x1 -> x0, blocking collectives: 58.6 us -> none  [local(): lax.all_to_all(send, 'outer', split_axis=0, concat_axis=0, tiled=True)]
    all_to_all x1 -> x0, waiting for transfers between devices: 28.1 us -> none  [local(): lax.all_to_all(answered, 'outer', split_axis=0, concat_axis=0, tiled=True)]
    psum x1 -> x0, waiting for transfers between devices: 21.7 us -> none  [local(): summed = lax.psum(total.astype(jnp.bfloat16), 'hid').astype(jnp.float32)]
    dot_general x2 -> x0, matrix products: 19.5 us -> none  [the longest x1 11.9 us: slice_terms(): return jnp.dot(hidden, down_piece, preferred_element_type=jnp.float32)]
    scatter x1 -> x0, local copies, waits for them, and re-layouts: 9.2 us -> none  [local(): jnp.zeros((experts * capacity, columns), jnp.bfloat16).at[slots]]
    all_to_all x1 -> x0, starting transfers between devices: 4.86 us -> none  [local(): lax.all_to_all(answered, 'outer', split_axis=0, concat_axis=0, tiled=True)]
  transfers between devices with their start and end apart: 5 -> 0, of which waited for: 5 -> 0; matrix products, arithmetic and copies ran while one was open for 5% -> 0% of each run, Pallas kernels for 0% -> 0%
where the time goes in v1:
time: 86.1 us; the launch traced here: 85.8 us
  Pallas kernels  81.2 us (94%)
  local copies, waits for them, and re-layouts  4.63 us (5%)
    pallas_call x1, Pallas kernels, local_kernel(): pl.pallas_call(functools.partial(layer_kernel, tuple(rounds), pieces), ou...  81.2 us
    unnamed x3, local copies, waits for them, and re-layouts  4.63 us

profile of v1, /device:TPU:0, one launch (start us, length us, event | category | flops | bytes accessed | tf_op | source)
XLA Modules:
  0.0 85.8 jit_solution(8395044020944252261)
XLA Ops:
  0.0 1.4 %copy.7.routes = s32[128,2]{1,0:T(8,128)} copy(s32[128,2]{0,1:T(2,128)} %param.7) | data formatting | bytes 2048 | tf_op args[1]
  1.4 1.4 %copy.8.scores = f32[128,2]{1,0:T(8,128)} copy(f32[128,2]{0,1:T(2,128)} %param.8) | data formatting | bytes 2048 | tf_op args[2]
  2.8 81.2 %shard_map.64 = bf16[128,1792]{1,0:T(8,128)(2,1)} custom-call(bf16[128,3584]{1,0:T(8,128)(2,1)} %tok.1, s32[128,2]{1,0:T(8,128)} %copy.7.routes, f32[128,2]{1,0:T(8,128)} %copy.8.scores, bf16[1,512,3584]{2,1,0:T(8,128)(2,1)} %gate_hbm.1, bf16[1,512,3584]{2,1,0:T(8,128)(2,1)} %up_hbm.1, bf16[1,512,3584]{2,1,0:T(8,128)(2,1)} %down_hbm.1), custom_call_target="tpu_custom_call" | custom-call | flops 7046430720 | bytes 11010048 | tf_op jit(solution)/shard_map/pallas_call | solution.py:327
  84.0 1.8 %copy.10 = bf16[128,1792]{1,0:T(8,128)(2,1)} copy(bf16[128,1792]{1,0:T(8,128)(2,1)} %shard_map.64) | data formatting | bytes 917504

commit v2 on v1

--- a/solution.py
+++ b/solution.py
@@ -98,24 +98,23 @@
     for peer in peers:
         pl.semaphore_signal(barrier, inc=1, device_id=peer, device_id_type=MESH)
 
-    tokens = routes.shape[0]
-    below = lax.broadcasted_iota(jnp.int32, (tokens, tokens), 1) < lax.broadcasted_iota(
-        jnp.int32, (tokens, tokens), 0)
-    below = jnp.where(below, 1.0, 0.0).astype(bf16)
-    weight = route_scale * scores[...] / (scores[:, 0:1] + scores[:, 1:2])
+    tokens = routes.shape[1]
+    above = lax.broadcasted_iota(jnp.int32, (tokens, tokens), 0) < lax.broadcasted_iota(
+        jnp.int32, (tokens, tokens), 1)
+    above = jnp.where(above, 1.0, 0.0).astype(bf16)
+    weight = route_scale * scores[...] / (scores[0:1, :] + scores[1:2, :])
     places, mixes = [], []
     start = 0
     for c in rounds:
-        wide = (tokens, steps * c)
-        lane = lax.broadcasted_iota(jnp.int32, wide, 1)
-        expert = lane // c
-        first = routes[:, 0:1] == expert
-        second = routes[:, 1:2] == expert
+        line = lax.broadcasted_iota(jnp.int32, (steps * c, tokens), 0)
+        expert = line // c
+        first = routes[0:1, :] == expert
+        second = routes[1:2, :] == expert
         named = jnp.where(first | second, 1.0, 0.0)
-        rank = jnp.dot(below, named.astype(bf16), preferred_element_type=f32)
-        slot = (lane - expert * c + start).astype(f32)
+        rank = jnp.dot(named.astype(bf16), above, preferred_element_type=f32)
+        slot = (line - expert * c + start).astype(f32)
         place = jnp.where(rank == slot, named, 0.0)
-        mix = place * (jnp.where(first, weight[:, 0:1], 0.0) + jnp.where(second, weight[:, 1:2], 0.0))
+        mix = place * (jnp.where(first, weight[0:1, :], 0.0) + jnp.where(second, weight[1:2, :], 0.0))
         mix_high = mix.astype(bf16)
         places.append(place.astype(bf16))
         mixes.append((mix_high, (mix - mix_high.astype(f32)).astype(bf16)))
@@ -130,33 +129,41 @@
 
     work = [(r, p) for r in range(len(rounds)) for p in range(pieces)]
     to_expert, across, beside, beside2, sum_hid, sum_blk, back = {}, {}, {}, {}, {}, {}, {}
+    across_own, sum_blk_own = {}, {}
     for n, (r, p) in enumerate(work):
         bufs, key = buffers[r], (r, p)
         rows = bufs["rows"]
         to_expert[key] = [
-            remote(bufs["send"].at[p, where[d]], rows.at[p, h, x, z], z_s.at[n, d], z_r.at[n, d], {"outer": where[d]})
+            remote(bufs["send"].at[p, where[d]], rows.at[p, h, x, d], z_s.at[n, d], z_r.at[n, d], {"outer": where[d]})
             for d in SEND_ORDER]
-        across[key] = remote(rows.at[p, h, x], rows.at[p, h, x], sem_s.at[0, n], sem_r.at[0, n], {"blk": ox})
+        far = pl.ds(1, steps - 1)
+        across[key] = remote(
+            rows.at[p, h, x, far], rows.at[p, h, x, far], sem_s.at[0, n], sem_r.at[0, n], {"blk": ox})
+        across_own[key] = remote(
+            rows.at[p, h, x, 0], rows.at[p, h, x, 0], sem_s.at[5, n], sem_r.at[5, n], {"blk": ox})
         beside[key] = remote(rows.at[p, h, x], rows.at[p, h, x], sem_s.at[1, n], sem_r.at[1, n], {"hid": oh})
         beside2[key] = remote(rows.at[p, h, ox], rows.at[p, h, ox], sem_s.at[2, n], sem_r.at[2, n], {"hid": oh})
         sum_hid[key] = remote(bufs["a_send"].at[p], bufs["a_recv"].at[p], sem_s.at[3, n], sem_r.at[3, n], {"hid": oh})
-        sum_blk[key] = remote(bufs["b_send"].at[p], bufs["b_recv"].at[p], sem_s.at[4, n], sem_r.at[4, n], {"blk": ox})
+        sum_blk[key] = remote(
+            bufs["b_send"].at[p, far], bufs["b_recv"].at[p, far], sem_s.at[4, n], sem_r.at[4, n], {"blk": ox})
+        sum_blk_own[key] = remote(
+            bufs["b_send"].at[p, 0], bufs["b_recv"].at[p, 0], sem_s.at[6, n], sem_r.at[6, n], {"blk": ox})
         back[key] = [
-            remote(bufs["c_send"].at[p, where[d]], bufs["ret"].at[p, z], back_s.at[n, d], back_r.at[n, d], {"outer": where[d]})
+            remote(bufs["c_send"].at[p, d], bufs["ret"].at[p, z], back_s.at[n, d], back_r.at[n, d], {"outer": where[d]})
             for d in SEND_ORDER]
 
     load_tok.wait()
 
     def build(r, p):
-        sent = lax.dot_general(
-            places[r], tokv[:, p * piece:(p + 1) * piece], (((0,), (0,)), ((), ())), preferred_element_type=f32)
+        sent = jnp.dot(places[r], tokv[:, p * piece:(p + 1) * piece], preferred_element_type=f32)
         buffers[r]["send"][p] = sent.astype(bf16).reshape(steps, rounds[r], piece)
         if (r, p) == work[0]:
             pl.semaphore_wait(barrier, len(peers))
         if work.index((r, p)) < WINDOW:
             for copy in to_expert[r, p]:
                 copy.start()
-        buffers[r]["rows"][p, h, x, z] = buffers[r]["send"][p, z]
+        buffers[r]["rows"][p, h, x, 0] = buffers[r]["send"][p, z]
+        across_own[r, p].start()
 
     def forward(r, p):
         n = work.index((r, p)) + WINDOW
@@ -169,6 +176,7 @@
         beside[r, p].start()
 
     def forward2(r, p):
+        across_own[r, p].wait_recv()
         across[r, p].wait_recv()
         beside2[r, p].start()
 
@@ -223,16 +231,22 @@
         sum_hid[r, p].wait_recv()
         bufs["b_send"][p] = (bufs["own"][p, ox] + bufs["a_recv"][p, ox].astype(f32)).astype(bf16)
         sum_blk[r, p].start()
+        if p == pieces - 1:
+            for q in range(pieces):
+                sum_blk_own[r, q].start()
         bufs["own"][p, x] = bufs["own"][p, x] + bufs["a_recv"][p, x].astype(f32)
 
     def reduce_blk(r, p):
         bufs = buffers[r]
         sum_blk[r, p].wait_recv()
-        total = (bufs["own"][p, x] + bufs["b_recv"][p].astype(f32)).astype(bf16)
-        bufs["c_send"][p] = total.reshape(bufs["c_send"].shape[1:])
+        bufs["c_send"][p, 1:] = (bufs["own"][p, x, 1:] + bufs["b_recv"][p, 1:].astype(f32)).astype(bf16)
         for copy in back[r, p]:
             copy.start()
-        bufs["ret"][p, z] = bufs["c_send"][p, z]
+
+    def reduce_own(r, p):
+        bufs = buffers[r]
+        sum_blk_own[r, p].wait_recv()
+        bufs["ret"][p, z] = (bufs["own"][p, x, 0] + bufs["b_recv"][p, 0].astype(f32)).astype(bf16)
 
     def combine(r, p):
         if r < len(rounds) - 1:
@@ -243,7 +257,7 @@
                 copy.wait_recv()
             result = buffers[q]["ret"][p].reshape(steps * rounds[q], piece)
             for mix in mixes[q]:
-                term = jnp.dot(mix, result, preferred_element_type=f32)
+                term = lax.dot_general(mix, result, (((0,), (0,)), ((), ())), preferred_element_type=f32)
                 value = term if value is None else value + term
         out[:, p * piece:(p + 1) * piece] = value.astype(bf16)
 
@@ -254,7 +268,11 @@
         return lines
 
     going = [staggered(r, (forward, forward2, compute)) for r in range(len(rounds))]
-    coming = [staggered(r, (down, reduce_hid, reduce_blk, combine)) for r in range(len(rounds))]
+    coming = [
+        staggered(r, (down, reduce_hid, reduce_blk))
+        + [[(reduce_own, r, p), (combine, r, p)] for p in range(pieces)]
+        for r in range(len(rounds))
+    ]
     plan = [(build, 0, p) for p in range(pieces)]
     for load in loads:
         plan.append((lambda r, p, load=load: load.start(), 0, 0))
@@ -272,7 +290,7 @@
     for key in work:
         for copy in to_expert[key] + back[key]:
             copy.wait_send()
-        for group in (across, beside, beside2, sum_hid, sum_blk):
+        for group in (across, across_own, beside, beside2, sum_hid, sum_blk, sum_blk_own):
             group[key].wait_send()
 
 
@@ -299,11 +317,11 @@
             "gate": pltpu.VMEM((2 * steps * c, units), f32),
             "up": pltpu.VMEM((2 * steps * c, units), f32),
             "hidden": pltpu.VMEM((2 * steps * c, units), bf16),
-            "own": pltpu.VMEM((pieces, 2, steps * c, piece), f32),
-            "a_send": pltpu.VMEM((pieces, 2, steps * c, piece), bf16),
-            "a_recv": pltpu.VMEM((pieces, 2, steps * c, piece), bf16),
-            "b_send": pltpu.VMEM((pieces, steps * c, piece), bf16),
-            "b_recv": pltpu.VMEM((pieces, steps * c, piece), bf16),
+            "own": pltpu.VMEM((pieces, 2, steps, c, piece), f32),
+            "a_send": pltpu.VMEM((pieces, 2, steps, c, piece), bf16),
+            "a_recv": pltpu.VMEM((pieces, 2, steps, c, piece), bf16),
+            "b_send": pltpu.VMEM((pieces, steps, c, piece), bf16),
+            "b_recv": pltpu.VMEM((pieces, steps, c, piece), bf16),
             "c_send": pltpu.VMEM((pieces, steps, c, piece), bf16),
             "ret": pltpu.VMEM((pieces, steps, c, piece), bf16),
         })
@@ -318,8 +336,8 @@
         dma((4,)),
         dma((number, steps)),
         dma((number, steps)),
-        dma((5, number)),
-        dma((5, number)),
+        dma((7, number)),
+        dma((7, number)),
         dma((number, steps)),
         dma((number, steps)),
     ]
@@ -333,7 +351,7 @@
         compiler_params=pltpu.CompilerParams(
             collective_id=0, has_side_effects=True, vmem_limit_bytes=56 * 1024 * 1024),
         cost_estimate=pl.CostEstimate(flops=2 * macs, bytes_accessed=6 * units * width, transcendentals=0),
-    )(tokens, routes, scores, gate_weight, up_weight, down_weight)
+    )(tokens, routes.T, scores.T, gate_weight, up_weight, down_weight)
 
 
 def solution(mesh):

time: 86.1 us -> 78.6 us (0.913)
  Pallas kernels: 81.2 us -> 76.6 us
  local copies, waits for them, and re-layouts: 4.63 us -> 1.82 us
    pallas_call x1, Pallas kernels: 81.2 us -> 76.6 us  [local_kernel(): pl.pallas_call(functools.partial(layer_kernel, tuple(rounds), pieces), ou...]
    unnamed x3 -> x1, local copies, waits for them, and re-layouts: 4.63 us -> 1.82 us
where the time goes in v2:
time: 78.6 us; the launch traced here: 78.4 us
  Pallas kernels  76.6 us (97%)
  local copies, waits for them, and re-layouts  1.82 us (2%)
    pallas_call x1, Pallas kernels, local_kernel(): pl.pallas_call(functools.partial(layer_kernel, tuple(rounds), pieces), ou...  76.6 us
    unnamed x1, local copies, waits for them, and re-layouts  1.82 us

profile of v2, /device:TPU:0, one launch (start us, length us, event | category | flops | bytes accessed | tf_op | source)
XLA Modules:
  0.0 78.4 jit_solution(15423320862854937331)
XLA Ops:
  0.0 76.6 %shard_map.64 = bf16[128,1792]{1,0:T(8,128)(2,1)} custom-call(bf16[128,3584]{1,0:T(8,128)(2,1)} %tok.1, s32[2,128]{1,0:T(2,128)} %bitcast.2, f32[2,128]{1,0:T(2,128)} %bitcast.3, bf16[1,512,3584]{2,1,0:T(8,128)(2,1)} %gate_hbm.1, bf16[1,512,3584]{2,1,0:T(8,128)(2,1)} %up_hbm.1, bf16[1,512,3584]{2,1,0:T(8,128)(2,1)} %down_hbm.1), custom_call_target="tpu_custom_call" | custom-call | flops 7046430720 | bytes 11010048 | tf_op jit(solution)/shard_map/pallas_call | solution.py:345
  76.6 1.8 %copy.8 = bf16[128,1792]{1,0:T(8,128)(2,1)} copy(bf16[128,1792]{1,0:T(8,128)(2,1)} %shard_map.64) | data formatting | bytes 917504

commit v3 on v2

--- a/solution.py
+++ b/solution.py
@@ -10,7 +10,7 @@
 PIECES = 7
 WINDOW = 2
 ROUND_PARTS = (1,)
-SEND_ORDER = (2, 3, 1)
+SEND_ORDER = (3, 2, 1)
 
 
 def slice_terms(rows, gate_piece, up_piece, down_piece):

time: 78.6 us -> 78.3 us (level)
  no operation moved by 1% of the time
where the time goes in v3:
time: 78.3 us; the launch traced here: 78.1 us
  Pallas kernels  76.2 us (97%)
  local copies, waits for them, and re-layouts  1.82 us (2%)
    pallas_call x1, Pallas kernels, local_kernel(): pl.pallas_call(functools.partial(layer_kernel, tuple(rounds), pieces), ou...  76.2 us
    unnamed x1, local copies, waits for them, and re-layouts  1.82 us

profile of v3, /device:TPU:0, one launch (start us, length us, event | category | flops | bytes accessed | tf_op | source)
XLA Modules:
  0.0 78.1 jit_solution(10978241728374049787)
XLA Ops:
  0.0 76.2 %shard_map.64 = bf16[128,1792]{1,0:T(8,128)(2,1)} custom-call(bf16[128,3584]{1,0:T(8,128)(2,1)} %tok.1, s32[2,128]{1,0:T(2,128)} %bitcast.2, f32[2,128]{1,0:T(2,128)} %bitcast.3, bf16[1,512,3584]{2,1,0:T(8,128)(2,1)} %gate_hbm.1, bf16[1,512,3584]{2,1,0:T(8,128)(2,1)} %up_hbm.1, bf16[1,512,3584]{2,1,0:T(8,128)(2,1)} %down_hbm.1), custom_call_target="tpu_custom_call" | custom-call | flops 7046430720 | bytes 11010048 | tf_op jit(solution)/shard_map/pallas_call | solution.py:345
  76.3 1.8 %copy.8 = bf16[128,1792]{1,0:T(8,128)(2,1)} copy(bf16[128,1792]{1,0:T(8,128)(2,1)} %shard_map.64) | data formatting | bytes 917504
